TPU v7x, 32 devices: a whole 2x2x4 slice. The times are simulated.
32 devices in a mesh: groups: 2 (over x), wide: 4 (over y, core), narrow: 4 (over z).
Axes of the slice: x: 2, y: 2, z: 4, core: 2. Of those that a mesh axis runs over, the one named last changes fastest.
Arguments:
- activations: bfloat16 [8, 128, 8192], P('groups', 'wide', 'narrow'), parts along dimension 0, may hold values from -6 to 6
- out_grads: bfloat16 [8, 128, 16384], P('groups', 'narrow', 'wide'), parts along dimension 0, may hold values from -6 to 6
- sign_bits: int32 [512, 16384], P('narrow', 'wide'), may hold values from 0 to 65535
- kept_row: int32 [4096], replicated, may hold values from 0 to 8191
- kept_col: int32 [4096], replicated, may hold values from 0 to 16383
Outputs:
- sketch: float32 [8, 4096], P('groups', ('wide', 'narrow')), parts along dimension 0
There are 2 independent parts, one for each index of `groups`. A program takes and returns all parts, laid end to end along the dimension named above; an argument that names none is the same for every part. Nothing has to cross between parts.
All inputs are finite; a program needn't handle non-finite values.
Results may differ from a plain program's by a relative error of at most 0.005.
Values may be sent and summed in bfloat16 or wider, within the bound.
No kernel may reach another device: no remote copies, remote signals or barrier semaphores. Data moves between devices by JAX's collectives and lax.ppermute only.
A program may use at most 512 MiB of HBM per device.

v0:
```python
import math

import jax
import jax.numpy as jnp
from jax import lax
from jax.sharding import PartitionSpec as P

D = 8192
FF = 16384
HLOW = 128
SEQ = 128


def parity_sign(first, second):
    folded = first & second
    folded = folded ^ folded >> 16
    folded = folded ^ folded >> 8
    folded = folded ^ folded >> 4
    folded = folded ^ folded >> 2
    folded = folded ^ folded >> 1
    return (1 - 2 * (folded & 1)).astype(jnp.float32)


def sylvester(order):
    index = jnp.arange(order, dtype=jnp.int32)
    return parity_sign(index[:, None], index[None, :])


def local(activations, out_grads, sign_bits, kept_row, kept_col):
    narrow_idx = lax.axis_index("narrow")
    wide_idx = lax.axis_index("wide")
    count = activations.shape[0]
    row_len = activations.shape[2]
    col_len = out_grads.shape[2]
    x_panel = lax.all_gather(activations, "wide", axis=1, tiled=True)
    grad = jnp.einsum(
        "etr,etc->erc",
        x_panel,
        lax.all_gather(out_grads, "narrow", axis=1, tiled=True),
        preferred_element_type=jnp.float32,
    )
    shifts = jnp.arange(16, dtype=jnp.int32)
    bits = (jnp.right_shift(sign_bits[:, None, :], shifts[None, :, None]) & 1).reshape(
        row_len, col_len
    )
    signed = ((1.0 - 2.0 * bits.astype(jnp.float32))[None, :, :] * grad).astype(jnp.bfloat16)
    row_high = row_len // HLOW
    col_high = col_len // HLOW
    h_low = sylvester(HLOW).astype(jnp.bfloat16)
    colmix = jnp.einsum(
        "erhl,lm->erhm",
        signed.reshape(count, row_len, col_high, HLOW),
        h_low,
        preferred_element_type=jnp.float32,
    ).astype(jnp.bfloat16)
    rowmix = jnp.einsum(
        "eaqhm,sq->eashm",
        colmix.reshape(count, row_high, HLOW, col_high, HLOW),
        h_low,
        preferred_element_type=jnp.float32,
    ).astype(jnp.bfloat16)
    picked = rowmix[:, :, kept_row % HLOW, :, kept_col % HLOW].astype(jnp.float32)
    row_ids = narrow_idx * row_high + jnp.arange(row_high, dtype=jnp.int32)
    col_ids = wide_idx * col_high + jnp.arange(col_high, dtype=jnp.int32)
    row_coeff = parity_sign((kept_row // HLOW)[:, None], row_ids[None, :])
    col_coeff = parity_sign((kept_col // HLOW)[:, None], col_ids[None, :])
    weighted = picked * row_coeff[:, None, :, None] * col_coeff[:, None, None, :]
    terms = jnp.transpose(jnp.sum(weighted, axis=(2, 3)))
    summed = lax.psum_scatter(terms, ("wide", "narrow"), scatter_dimension=1, tiled=True)
    return summed * (1.0 / math.sqrt(D * FF * SEQ))


def solution(mesh):
    return jax.shard_map(
        local,
        mesh=mesh,
        in_specs=(
            P("groups", "wide", "narrow"),
            P("groups", "narrow", "wide"),
            P("narrow", "wide"),
            P(),
            P(),
        ),
        out_specs=P("groups", ("wide", "narrow")),
        check_vma=False,
    )
```

profile of v0, /device:TPU:0, one launch (start us, length us, event | category | flops | bytes accessed | tf_op | source)
XLA Modules:
  0.0 1777.8 jit_solution(2818783064071576896)
XLA Ops:
  6.5 0.0 copy-start.3
  6.5 0.0 copy-start.4
  6.5 0.0 all-gather.3.cloned.1.call-start
  6.5 0.7 all-gather.3.cloned.1.call-update
  7.3 0.0 all-gather.5.cloned.1.call-start
  7.3 0.7 all-gather.5.cloned.1.call-update
  8.0 0.0 reduce-scatter.4.cloned.1.call-start
  8.1 0.1 shift_right_arithmetic.157
  8.2 13.4 fusion.13
  21.6 0.0 copy-done.3
  21.6 0.0 copy-done.4
  21.6 0.6 add_select_fusion.1
  22.3 0.9 fusion.22
  23.2 1.1 fusion.18
  24.3 10.0 all-gather.3.cloned.1.call-done
  34.2 82.4 %all-gather.5.cloned.1.call-done = bf16[4,128,4096]{2,1,0:T(8,128)(2,1)} async-done(((bf16[4,32,4096]{2,1,0:T(8,128)(2,1)}), bf16[4,128,4096]{2,1,0:T(8,128)(2,1)}) %all-gather.5.cloned.1.call-update) | async-done | bytes 4194320 | tf_op jit(solution)/shard_map/all_gather | solution.py:39
  116.6 38.6 %fusion.14 = bf16[4,256,32,8,128]{4,3,2,1,0:T(8,128)(2,1)} fusion(bf16[4,128,2048]{2,1,0:T(8,128)(2,1)} %all-gather.3.cloned.1.call-done, bf16[4,128,4096]{2,1,0:T(8,128)(2,1)} %all-gather.5.cloned.1.call-done, f32[2048,4096]{1,0:T(8,128)} %fusion.13), kind=kOutput, calls=%fused_computation.15 | convolution fusion | flops 8657043456 | bytes 106954752 | tf_op jit(solution)/shard_map/etr,etc->erc/dot_general | solution.py:36
  155.2 46.0 %fusion.5 = bf16[4,2048,32,128]{3,1,2,0:T(8,128)(2,1)} fusion(bf16[4,256,32,8,128]{4,3,2,1,0:T(8,128)(2,1)} %fusion.14), kind=kOutput, calls=%fused_computation.8 | convolution fusion | flops 8623751168 | bytes 134217728 | tf_op jit(solution)/shard_map/erhl,lm->erhm/dot_general | solution.py:50
  201.2 46.1 %convert_bitcast_fusion = bf16[4,16,128,32,128]{4,2,3,1,0:T(8,128)(2,1)} fusion(bf16[4,16,128,32,128]{4,2,1,3,0:T(8,128)(2,1)} %bitcast.5), kind=kOutput, calls=%fused_computation.7 | convolution fusion | flops 8623751168 | bytes 134217728 | tf_op jit(solution)/shard_map/eaqhm,sq->eashm/dot_general | solution.py:56
  247.3 59.9 %copy.13 = bf16[4,16,128,32,128]{4,3,2,1,0:T(8,128)(2,1)} copy(bf16[4,16,128,32,128]{4,2,3,1,0:T(8,128)(2,1)} %convert_bitcast_fusion) | data formatting | bytes 134217728 | tf_op jit(solution)/shard_map/convert_element_type | solution.py:61
  307.1 0.0 copy-done
  307.1 0.0 copy-start.1
  307.2 0.0 copy-start.2
  307.2 1392.8 %gather_fusion = bf16[4096,4,16,32]{0,3,2,1:T(8,128)(2,1)} fusion(bf16[4,16,128,32,128]{4,3,2,1,0:T(8,128)(2,1)} %copy.13, s32[4096]{0:T(1024)S(1)} %copy-done), kind=kCustom, calls=%fused_computation | custom fusion | bytes 33587200 | tf_op jit(solution)/shard_map/gather | solution.py:62
  1699.9 0.0 copy-done.1
  1699.9 0.0 copy-done.2
  1699.9 7.4 multiply_reduce_fusion
  1707.4 2.0 copy.16
  1709.4 0.0 reduce-scatter.4.cloned.1.call-update
  1709.4 60.3 %reduce-scatter.4.cloned.1.call-done = f32[256,4]{1,0:T(8,128)} async-done(((f32[4096,4]{1,0:T(8,128)}), f32[256,4]{1,0:T(8,128)}) %reduce-scatter.4.cloned.1.call-update) | async-done | bytes 4112
  1769.7 1.0 copy.17
  1770.6 0.6 broadcast_multiply_fusion
  (4 shorter events, 0.0 us)
Async XLA Ops:
  6.5 15.1 copy-start.3
  6.5 15.1 copy-start.4
  6.5 27.7 %all-gather.3.cloned.1.call-start = ((), (), s32[]{:S(2)}) async-start(), calls=%async_computation.1 | async-start | bytes 2621440 | tf_op jit(solution)/shard_map/all_gather | solution.py:35
  7.3 109.3 %all-gather.5.cloned.1.call-start = ((), (), s32[]{:S(2)}) async-start(), calls=%async_computation.2 | async-start | bytes 5242880 | tf_op jit(solution)/shard_map/all_gather | solution.py:39
  8.0 1761.7 %reduce-scatter.4.cloned.1.call-start = ((), (), s32[]{:S(2)}) async-start(), calls=%async_computation.3 | async-start | bytes 2228224
  247.3 59.9 %copy-start = (s32[4096]{0:T(1024)S(1)}, s32[4096]{0:T(1024)}, u32[]{:S(2)}) copy-start(s32[4096]{0:T(1024)} %get-tuple-element.6) | copy-start | bytes 49156
  307.1 1392.8 %copy-start.1 = (f32[4096,32]{0,1:T(8,128)S(1)}, f32[4096,32]{0,1:T(8,128)}, u32[]{:S(2)}) copy-start(f32[4096,32]{0,1:T(8,128)} %fusion.18) | copy-start | bytes 1572868
  307.2 1392.8 %copy-start.2 = (f32[4096,16]{0,1:T(8,128)S(1)}, f32[4096,16]{0,1:T(8,128)}, u32[]{:S(2)}) copy-start(f32[4096,16]{0,1:T(8,128)} %fusion.22) | copy-start | bytes 786436
Sparse Core Ops, SparseCore 0:
  8.9 25.2 all-gather.2
  35.8 80.7 all-gather.4
  1709.5 60.0 reduce-scatter.3
where the time goes:
time: 1780 us
  local copies, waits for them, and re-layouts  1460 us (82%)
  waiting for transfers between devices  154 us (9%)
  matrix products  131 us (7%)
  other arithmetic  24.2 us (1%)
    gather x1, local copies, waits for them, and re-layouts, local(): rowmix[:, :, kept_row % HLOW, :, kept_col % HLOW].astype(jnp.float32)  1390 us
    all_gather x1, waiting for transfers between devices, local(): lax.all_gather(out_grads, 'narrow', axis=1, tiled=True)  82.4 us
    unnamed x4, waiting for transfers between devices  61.7 us
    convert_element_type x1, local copies, waits for them, and re-layouts, local(): rowmix = jnp.einsum('eaqhm,sq->eashm', colmix.reshape(count, row_high, HL...  59.9 us
    dot_general x1, matrix products, local(): jnp.einsum('eaqhm,sq->eashm', colmix.reshape(count, row_high, HLOW, col_h...  46.1 us
    dot_general x1, matrix products, local(): jnp.einsum('erhl,lm->erhm', signed.reshape(count, row_len, col_high, HLOW...  46 us
    dot_general x1, matrix products, local(): jnp.einsum('etr,etc->erc', x_panel, lax.all_gather(out_grads, 'narrow', a...  38.6 us
  transfers between devices with their start and end apart: 3, of which 3 were waited for; matrix products, arithmetic and copies ran while one was open for 1% of the time, Pallas kernels for 0%

commit v1 on v0

v1 whole, which is shorter than its diff:
```python
import functools
import math

import jax
import jax.numpy as jnp
from jax import lax
from jax.experimental import pallas as pl
from jax.experimental.pallas import tpu as pltpu
from jax.sharding import PartitionSpec as P

D = 8192
FF = 16384
SEQ = 128
BLK = 256
LOW = 8
GROUPS = BLK // LOW
LANES = 128
TILE = 128
WIDE = 512
ROW_HIGH = (D // BLK).bit_length() - 1
COL_BITS = FF.bit_length() - 1


def parity_sign(first, second):
    folded = first & second
    folded = folded ^ folded >> 8
    folded = folded ^ folded >> 4
    folded = folded ^ folded >> 2
    folded = folded ^ folded >> 1
    return (1 - 2 * (folded & 1)).astype(jnp.bfloat16)


def in_groups(kept_row, kept_col):
    key = ((kept_row & (BLK - 1)) << ROW_HIGH | kept_row // BLK) << COL_BITS | kept_col
    return lax.sort((key, lax.iota(jnp.int32, key.shape[0])), num_keys=1)


def plan(key, order, base, na, nh):
    k = key.shape[0]
    col = key & (FF - 1)
    row_low = key >> (COL_BITS + ROW_HIGH)
    group = row_low // LOW
    code = (key >> COL_BITS) & (D // BLK - 1) | (col // BLK) << ROW_HIGH
    d = jnp.arange(LANES, dtype=jnp.int32)

    def bits_of(d):
        return (d // LOW) % na | d // (LOW * na) << ROW_HIGH

    hit = (row_low & (LOW - 1))[:, None] == (d % LOW)[None, :]
    pick = jnp.where(hit, parity_sign(code[:, None], (base ^ bits_of(d))[None, :]), 0).astype(jnp.bfloat16)
    tops = (na * nh * LOW // LANES).bit_length() - 1
    top = bits_of(LANES << jnp.arange(max(tops, 1), dtype=jnp.int32))
    flip = jnp.broadcast_to(parity_sign(code[None, :], top[:, None])[:, :, None], (max(tops, 1), k, LANES))
    lane = parity_sign((col & (BLK - 1))[:, None], jnp.arange(BLK, dtype=jnp.int32)[None, :])
    tiles = k // TILE
    low_hot = ((order % LANES)[:, None] == d[None, :]).astype(jnp.bfloat16)
    high = jnp.arange(k // LANES, dtype=jnp.int32)
    high_hot = ((order // LANES)[None, :] == high[:, None]).astype(jnp.bfloat16)
    ends = jnp.sum((group[None, :] <= jnp.arange(GROUPS, dtype=jnp.int32)[:, None]).astype(jnp.int32), axis=1)
    cuts = jnp.sort(jnp.concatenate([jnp.arange(tiles, dtype=jnp.int32) * TILE, ends[:-1]]))
    item_tile = jnp.minimum(cuts // TILE, tiles - 1)
    item_group = jnp.minimum(jnp.sum((ends[None, :] <= cuts[:, None]).astype(jnp.int32), axis=1), GROUPS - 1)
    items = jnp.stack([item_tile, item_group, cuts - item_tile * TILE])
    return items, pick, flip, lane, low_hot, high_hot


def halve(x):
    coarse = x.astype(jnp.bfloat16)
    return coarse, (x - coarse.astype(jnp.float32)).astype(jnp.bfloat16)


def body(parts, na, nc, steps, tops, unroll, items, place, a_ref, *refs):
    g_refs = refs[:parts]
    words_ref, h_ref, pick_hbm, flip_hbm, lane_hbm, low_hbm, high_ref, out_ref, at, w, pick, flip, lane, low, part, spread, sems = refs[parts:]
    step = pl.program_id(0)
    pairs = ((pick_hbm, pick), (flip_hbm, flip), (lane_hbm, lane), (low_hbm, low))
    copies = [pltpu.make_async_copy(s, d, sems.at[i]) for i, (s, d) in enumerate(pairs)]

    @pl.when(step == 0)
    def _():
        for c in copies:
            c.start()
        blocks, _, _, span = a_ref.shape
        for j in range(blocks):
            tokens = jnp.concatenate([a_ref[j, place[0] ^ s] for s in range(parts)], axis=0)
            at[j * span:(j + 1) * span, :] = tokens.T

    depth = na * LOW
    shift = 31 - lax.broadcasted_iota(jnp.int32, (BLK // 16, 16, BLK), 1)
    for c in range(nc):
        cols = slice(c * BLK, (c + 1) * BLK)
        grads_out = jnp.concatenate([g[:, cols] for g in g_refs], axis=0)
        for a in range(0, na, 2):
            halves = []
            for b in (a, a + 1):
                rows = slice(b * BLK, (b + 1) * BLK)
                grad = jnp.dot(at[rows, :], grads_out, preferred_element_type=jnp.float32)
                words = words_ref[b * BLK // 16:(b + 1) * BLK // 16, cols]
                marks = (jnp.broadcast_to(words[:, None, :], shift.shape) << shift).reshape(BLK, BLK)
                signed = jnp.where(marks < 0, -grad, grad).astype(jnp.bfloat16)
                mixed = jnp.dot(h_ref[...], signed, preferred_element_type=jnp.float32)
                halves.append(mixed.reshape(GROUPS, LOW, BLK))
            both = jnp.concatenate(halves, axis=1).astype(jnp.bfloat16)
            w[:, pl.ds(pl.multiple_of((step * nc + c) * depth + a * LOW, 2 * LOW), 2 * LOW), :] = both

    @pl.when(step == steps - 1)
    def _():
        for c in copies:
            c.wait()
        slot = lax.broadcasted_iota(jnp.int32, (TILE, LANES), 0)

        def item(i, carry):
            t, g = items[0, i], items[1, i]
            at_t = pl.ds(pl.multiple_of(t * TILE, TILE), TILE)
            signs = [pick[at_t, :]]
            for b in range(tops):
                signs += [s * flip[b, at_t, :] for s in signs]
            mixed = jnp.dot(jnp.concatenate(signs, axis=1), w[g], preferred_element_type=jnp.float32)
            mixed = mixed * lane[at_t, :].astype(jnp.float32)
            part[at_t, :] = jnp.where(slot >= items[2, i], mixed[:, :LANES] + mixed[:, LANES:], part[at_t, :])
            return carry

        lax.fori_loop(0, items.shape[1], item, 0, unroll=unroll)
        ones = jnp.ones((LANES, LANES), jnp.bfloat16)

        def back(t, carry):
            at_t = pl.ds(pl.multiple_of(t * TILE, TILE), TILE)
            value = sum(jnp.dot(x, ones, preferred_element_type=jnp.float32) for x in halve(part[at_t, :]))
            for i, x in enumerate(halve(value)):
                spread[i, at_t, :] = x * low[at_t, :]
            return carry

        lax.fori_loop(0, high_ref.shape[1] // TILE, back, 0, unroll=32)
        out_ref[...] = sum(jnp.dot(high_ref[...], spread[i], preferred_element_type=jnp.float32) for i in (0, 1))


def sketch_terms(items, place, a, example, g_parts, words, h, pick, flip, lane, low_hot, high_hot):
    blocks, parts, few, span = a.shape
    rows, cols = 16 * words.shape[0], words.shape[1]
    wide = min(cols, WIDE)
    steps = cols // wide
    na, nc = rows // BLK, wide // BLK
    k = pick.shape[0]
    depth = na * nc * steps * LOW
    tops = (depth // LANES).bit_length() - 1
    whole = lambda *shape: pl.BlockSpec(shape, lambda j, *s: (0,) * len(shape))
    hbm = pl.BlockSpec(memory_space=pl.ANY)
    return pl.pallas_call(
        functools.partial(body, parts, na, nc, steps, tops, 21),
        out_shape=jax.ShapeDtypeStruct((k // LANES, LANES), jnp.float32),
        grid_spec=pltpu.PrefetchScalarGridSpec(
            num_scalar_prefetch=2,
            grid=(steps,),
            in_specs=[whole(*a.shape)]
            + [pl.BlockSpec((None, few, wide), lambda j, *s: (example, 0, j))] * parts
            + [pl.BlockSpec((rows // 16, wide), lambda j, *s: (0, j)), whole(BLK, BLK)]
            + [hbm] * 4
            + [whole(*high_hot.shape)],
            out_specs=whole(k // LANES, LANES),
            scratch_shapes=[
                pltpu.VMEM((rows, a.shape[1] * few), jnp.bfloat16),
                pltpu.VMEM((GROUPS, depth, BLK), jnp.bfloat16),
                pltpu.VMEM(pick.shape, jnp.bfloat16),
                pltpu.VMEM(flip.shape, jnp.bfloat16),
                pltpu.VMEM(lane.shape, jnp.bfloat16),
                pltpu.VMEM(low_hot.shape, jnp.bfloat16),
                pltpu.VMEM((k, LANES), jnp.float32),
                pltpu.VMEM((2, k, LANES), jnp.bfloat16),
                pltpu.SemaphoreType.DMA((4,)),
            ],
        ),
        compiler_params=pltpu.CompilerParams(vmem_limit_bytes=52 << 20),
        cost_estimate=pl.CostEstimate(
            flops=2 * rows * wide * steps * 3 * BLK, bytes_accessed=2 * rows * wide * steps, transcendentals=0
        ),
    )(items, place, a, *g_parts, words, h, pick, flip, lane, low_hot, high_hot)


def local(sizes, share, activations, out_grads, sign_bits, kept_row, kept_col):
    wide_size, narrow_size = sizes["wide"], sizes["narrow"]
    n = lax.axis_index("narrow")
    wide_idx = lax.axis_index("wide")
    count = activations.shape[0]
    row_len = activations.shape[2]
    col_len = out_grads.shape[2] // share
    few = out_grads.shape[1]
    k = kept_row.shape[0]
    na = share * row_len // BLK
    nh = col_len // BLK

    def swap(x, s):
        return lax.ppermute(x, "narrow", [(j, j ^ s) for j in range(narrow_size)])

    def columns(x, s):
        return lax.dynamic_slice_in_dim(x, ((n ^ s) % share) * col_len, col_len, x.ndim - 1)

    def panel(shards):
        return lax.all_gather(jnp.stack(shards), "wide", axis=1, tiled=True)

    near = [activations[0]] + [swap(activations[0], s) for s in range(1, share)]
    panels = [panel(near)]
    words = [columns(sign_bits, 0)] + [swap(columns(sign_bits, s).astype(jnp.uint16), s) for s in range(1, share)]
    outs = out_grads[:1]
    grads = [(0, [columns(outs, 0)] + [swap(columns(outs, s), s) for s in range(1, narrow_size)])]
    key, order = in_groups(kept_row, kept_col)
    acts, outs, key, order, *_ = lax.optimization_barrier(
        (activations[1:], out_grads[1:], key, order, words[-1], near[-1])
    )
    words = jnp.concatenate([x.astype(jnp.int32) for x in words])
    others = [acts] + [swap(acts, s) for s in range(1, share)]
    rest = [columns(outs, 0)] + [swap(columns(outs, s), s) for s in range(1, narrow_size)]
    for e in range(count - 1):
        panels.append(panel([x[e] for x in others]))
        grads.append((e, rest))
    base = n * (row_len // BLK) | ((wide_idx * share + n % share) * nh) << ROW_HIGH
    factors = plan(key, order, base, na, nh)
    index = jnp.arange(BLK, dtype=jnp.int32)
    h = parity_sign(index[:, None], index[None, :])
    place = jnp.full((1,), n, jnp.int32)
    terms = []
    for e in range(count):
        a = panels[e].reshape(share, narrow_size, few, row_len)
        terms.append(sketch_terms(factors[0], place, a, *grads[e], words, h, *factors[1:]))
    owners = wide_size * narrow_size
    send = jnp.stack(terms).reshape(count, owners, k // owners).transpose(1, 0, 2)
    got = lax.all_to_all(send, ("wide", "narrow"), 0, 0, tiled=True)
    return jnp.sum(got, axis=0) * (1.0 / math.sqrt(D * FF * SEQ))


def solution(mesh):
    return jax.shard_map(
        functools.partial(local, dict(mesh.shape), 2),
        mesh=mesh,
        in_specs=(
            P("groups", "wide", "narrow"),
            P("groups", "narrow", "wide"),
            P("narrow", "wide"),
            P(),
            P(),
        ),
        out_specs=P("groups", ("wide", "narrow")),
        check_vma=False,
    )
```

time: 1780 us -> 161 us (0.09)
  local copies, waits for them, and re-layouts: 1460 us -> 7.04 us
  waiting for transfers between devices: 154 us -> 13.8 us
  matrix products: 131 us -> 0 us
  Pallas kernels: 0 us -> 75.1 us
    gather x1 -> x0, local copies, waits for them, and re-layouts: 1390 us -> none  [local(): rowmix[:, :, kept_row % HLOW, :, kept_col % HLOW].astype(jnp.float32)]
    dot_general x3 -> x0, matrix products: 131 us -> none  [the longest x1 46.1 us: local(): jnp.einsum('eaqhm,sq->eashm', colmix.reshape(count, row_high, HLOW, col_h...]
    all_gather x2 -> x4, waiting for transfers between devices: 92.3 us -> 0.07 us  [panel(): return lax.all_gather(jnp.stack(shards), 'wide', axis=1, tiled=True)]
    pallas_call x0 -> x4, Pallas kernels: none -> 75.1 us  [sketch_terms(): pl.pallas_call(functools.partial(body, parts, na, nc, steps, tops, 21), o...]
    unnamed x4, waiting for transfers between devices: 61.7 us -> 0.07 us
    convert_element_type x1 -> x0, local copies, waits for them, and re-layouts: 59.9 us -> none  [local(): rowmix = jnp.einsum('eaqhm,sq->eashm', colmix.reshape(count, row_high, HL...]
  transfers between devices with their start and end apart: 3 -> 13, of which waited for: 3 -> 2; matrix products, arithmetic and copies ran while one was open for 1% -> 18% of each run, Pallas kernels for 0% -> 35%
where the time goes in v1:
time: 161 us; the launch traced here: 160 us
  Pallas kernels  75.1 us (47%)
  other arithmetic  25.9 us (16%)
  waiting for transfers between devices  13.8 us (9%)
  starting transfers between devices  13.5 us (8%)
  between operations  13.4 us (8%)
  blocking collectives  11.3 us (7%)
  local copies, waits for them, and re-layouts  7.04 us (4%)
    pallas_call x4, Pallas kernels, sketch_terms(): pl.pallas_call(functools.partial(body, parts, na, nc, steps, tops, 21), o...  75.1 us
    ppermute x9, waiting for transfers between devices, swap(): return lax.ppermute(x, 'narrow', [(j, j ^ s) for j in range(narrow_size)])  13.7 us
    ppermute x9, starting transfers between devices, swap(): return lax.ppermute(x, 'narrow', [(j, j ^ s) for j in range(narrow_size)])  13.2 us
    all_to_all x1, blocking collectives, local(): got = lax.all_to_all(send, ('wide', 'narrow'), 0, 0, tiled=True)  11.3 us
    sort x1, other arithmetic, in_groups(): return lax.sort((key, lax.iota(jnp.int32, key.shape[0])), num_keys=1)  5.17 us
    convert_element_type x3, other arithmetic, parity_sign(): return (1 - 2 * (folded & 1)).astype(jnp.bfloat16)  3.5 us
  transfers between devices with their start and end apart: 13, of which 2 were waited for; matrix products, arithmetic and copies ran while one was open for 18% of the time, Pallas kernels for 35%

profile of v1, /device:TPU:0, one launch (start us, length us, event | category | flops | bytes accessed | tf_op | source)
XLA Modules:
  0.0 160.1 jit_solution(14296539340672105894)
XLA Ops:
  6.5 3.0 %constant_dynamic-slice_fusion.4 = (s32[128,2048]{1,0:T(8,128)}, u16[128,2048]{1,0:T(8,128)(2,1)}) fusion(s32[128,4096]{1,0:T(8,128)} %param.7, s32[]{:T(128)S(6)} %select_n.146, s32[]{:T(128)S(6)} %select_n.142), kind=kLoop, calls=%fused_computation.87 | loop fusion | flops 262144 | bytes 3670024 | tf_op jit(solution)/shard_map/dynamic_slice | solution.py:195
  9.5 3.0 %collective-permute-start = (u16[128,2048]{1,0:T(8,128)(2,1)}, u16[128,2048]{1,0:T(8,128)(2,1)S(1)}, u32[]{:S(2)}, u32[]{:S(2)}) collective-permute-start(u16[128,2048]{1,0:T(8,128)(2,1)} %get-tuple-element.23), channel_id=1, source_target_pairs={{0,1},{1,0},{2,3},{3,2},{4,5},{5,4},{6,7},{7,6},{8,9},{9,8},{10,11... | collective-permute-start | bytes 1572872 | tf_op jit(solution)/shard_map/ppermute | solution.py:192
  12.5 0.9 fusion.40
  13.6 0.8 constant_dynamic-slice_fusion.5
  14.4 1.9 %collective-permute-start.2 = (bf16[1,32,2048]{2,1,0:T(8,128)(2,1)}, bf16[1,32,2048]{2,1,0:T(8,128)(2,1)S(1)}, u32[]{:S(2)}, u32[]{:S(2)}) collective-permute-start(bf16[1,32,2048]{2,1,0:T(8,128)(2,1)} %get-tuple-element.38), channel_id=1, source_target_pairs={{0,1},{1,0},{2,3},{3,2},{4,5},{5,4},{6,7},{7,6},{8,9},{9,8},{10,11... | collective-permute-start | bytes 393224 | tf_op jit(solution)/shard_map/ppermute | solution.py:192
  16.3 2.6 %collective-permute-start.3 = (bf16[1,32,2048]{2,1,0:T(8,128)(2,1)}, bf16[1,32,2048]{2,1,0:T(8,128)(2,1)S(1)}, u32[]{:S(2)}, u32[]{:S(2)}) collective-permute-start(bf16[1,32,2048]{2,1,0:T(8,128)(2,1)} %get-tuple-element.37), channel_id=1, source_target_pairs={{0,2},{1,3},{2,0},{3,1},{4,6},{5,7},{6,4},{7,5},{8,10},{9,11},{10,... | collective-permute-start | bytes 393224 | tf_op jit(solution)/shard_map/ppermute | solution.py:192
  19.0 1.0 slice.34
  20.0 5.2 %sort.30 = (s32[4096]{0:T(1024)S(1)}, s32[4096]{0:T(1024)S(1)}) sort(s32[4096]{0:T(1024)S(1)} %fusion.21, s32[4096]{0:T(1024)S(1)} %iota.43), dimensions={0}, to_apply=%region_0.1 | sort | flops 49152 | bytes 65536 | tf_op jit(solution)/shard_map/sort | solution.py:35
  25.3 5.8 %collective-permute-done.1 = bf16[32,2048]{1,0:T(8,128)(2,1)S(1)} collective-permute-done((bf16[32,2048]{1,0:T(8,128)(2,1)S(1)}, bf16[32,2048]{1,0:T(8,128)(2,1)S(1)}, u32[]{:S(2)}, u32[]{:S(2)}) %collective-permute-start.1) | collective-permute-done | bytes 131104 | tf_op jit(solution)/shard_map/ppermute | solution.py:192
  31.1 0.7 pad_maximum_fusion
  32.0 1.1 constant_dynamic-slice_fusion
  33.1 2.0 %collective-permute-start.6 = (bf16[3,32,2048]{2,1,0:T(8,128)(2,1)}, bf16[3,32,2048]{2,1,0:T(8,128)(2,1)S(1)}, u32[]{:S(2)}, u32[]{:S(2)}) collective-permute-start(bf16[3,32,2048]{2,1,0:T(8,128)(2,1)} %get-tuple-element.26), channel_id=1, source_target_pairs={{0,1},{1,0},{2,3},{3,2},{4,5},{5,4},{6,7},{7,6},{8,9},{9,8},{10,11... | collective-permute-start | bytes 1179656 | tf_op jit(solution)/shard_map/ppermute | solution.py:192
  35.1 2.7 %fusion.8.refs_9_ = bf16[4096,128]{1,0:T(8,128)(2,1)} fusion(s32[4096]{0:T(1024)S(1)} %get-tuple-element.41), kind=kLoop, calls=%fused_computation.18 | loop fusion | flops 1048576 | bytes 1064960 | tf_op jit(solution)/shard_map/convert_element_type | solution.py:56
  38.0 0.2 convert_reduce_fusion
  38.2 7.9 %collective-permute-done.5 = bf16[3,32,2048]{2,1,0:T(8,128)(2,1)S(1)} collective-permute-done((bf16[3,32,2048]{2,1,0:T(8,128)(2,1)S(1)}, bf16[3,32,2048]{2,1,0:T(8,128)(2,1)S(1)}, u32[]{:S(2)}, u32[]{:S(2)}) %collective-permute-start.5) | collective-permute-done | bytes 393248 | tf_op jit(solution)/shard_map/ppermute | solution.py:192
  46.1 2.1 %collective-permute-start.7 = (bf16[3,32,2048]{2,1,0:T(8,128)(2,1)}, bf16[3,32,2048]{2,1,0:T(8,128)(2,1)S(1)}, u32[]{:S(2)}, u32[]{:S(2)}) collective-permute-start(bf16[3,32,2048]{2,1,0:T(8,128)(2,1)} %get-tuple-element.25), channel_id=1, source_target_pairs={{0,2},{1,3},{2,0},{3,1},{4,6},{5,7},{6,4},{7,5},{8,10},{9,11},{10,... | collective-permute-start | bytes 1179656 | tf_op jit(solution)/shard_map/ppermute | solution.py:192
  48.3 0.7 pad_maximum_fusion.3
  49.1 2.0 %sort.31 = (s32[63]{0:T(128)S(1)}, s32[63]{0:T(128)}) sort(s32[63]{0:T(128)S(1)} %pad_add_fusion.2, s32[63]{0:T(128)S(1)} %iota.44), dimensions={0}, to_apply=%region_2.3 | sort | flops 378 | bytes 1008 | tf_op jit(solution)/shard_map/jit(sort)/sort | solution.py:60
  51.3 2.5 %compare_select_fusion.refs_6_ = bf16[4096,128]{1,0:T(8,128)(2,1)} fusion(s32[128]{0:T(128)S(1)} %get-tuple-element.47, s32[4096]{0:T(1024)S(1)} %get-tuple-element.49, s32[128]{0:T(128)S(1)} %get-tuple-element.46, s32[4096]{0:T(1024)S(1)} %get-tuple-element.50), kind=kLoop, calls=%fused_computation.19 | loop fusion | flops 7864320 | bytes 1082368 | tf_op jit(solution)/shard_map/jit(_where)/select_n | solution.py:50
  53.8 0.7 pad_maximum_fusion.2
  54.6 0.2 all-gather.7.cloned.1.call-start
  54.9 2.8 %pad_add_fusion.refs_4_ = s32[256,2048]{1,0:T(8,128)} fusion(s32[128,2048]{1,0:T(8,128)S(1)} %convert_element_type.45, s32[128,2048]{1,0:T(8,128)} %get-tuple-element.22), kind=kLoop, calls=%fused_computation.16 | loop fusion | flops 524288 | bytes 4194304 | tf_op jit(solution)/shard_map/concatenate | solution.py:209
  57.7 3.2 %fusion.3.refs_8_ = bf16[4096,256]{1,0:T(8,128)(2,1)} fusion(s32[4096]{0:T(1024)S(1)} %get-tuple-element.51), kind=kLoop, calls=%fused_computation.7 | loop fusion | flops 13631488 | bytes 2113536 | tf_op jit(solution)/shard_map/convert_element_type | solution.py:30
  61.0 0.7 pad_maximum_fusion.1
  61.7 1.4 collective-permute-start.8
  63.2 3.2 %broadcast_in_dim.10.refs_7_ = bf16[3,4096,128]{2,1,0:T(8,128)(2,1)} broadcast(bf16[3,4096]{1,0:T(4,128)(2,1)S(1)} %fusion.17), dimensions={0,1} | broadcast | bytes 3170304 | tf_op jit(solution)/shard_map/broadcast_in_dim | solution.py:53
  66.3 18.4 %shard_map.55 = f32[32,128]{1,0:T(8,128)S(1)} custom-call(s32[3,63]{1,0:T(4,128)S(1)} %pad_add_fusion.1.items, s32[1]{0:T(128)} %bitcast.4.place, bf16[2,4,32,2048]{3,2,1,0:T(8,128)(2,1)S(1)} %bitcast.24, bf16[1,32,2048]{2,1,0:T(8,128)(2,1)S(1)} %get-tuple-element.39.refs_0_, bf16[1,32,2048]{2,1,0:T(8,128)(2,1)S(1)} %collective-permute-done.2.refs_1_, ...), custom_call_target="tpu_custom_call" | custom-call | flops 12884901888 | bytes 16777216 | tf_op jit(solution)/shard_map/pallas_call | solution.py:148
  84.8 19.0 %shard_map.58 = f32[32,128]{1,0:T(8,128)S(1)} custom-call(s32[3,63]{1,0:T(4,128)S(1)} %pad_add_fusion.1.items, s32[1]{0:T(128)} %bitcast.4.place, bf16[2,4,32,2048]{3,2,1,0:T(8,128)(2,1)} %bitcast.28, bf16[3,32,2048]{2,1,0:T(8,128)(2,1)S(1)} %get-tuple-element.27.refs_0_, bf16[3,32,2048]{2,1,0:T(8,128)(2,1)S(1)} %collective-permute-done.6.refs_1_, ...), custom_call_target="tpu_custom_call" | custom-call | flops 12884901888 | bytes 16777216 | tf_op jit(solution)/shard_map/pallas_call | solution.py:148
  103.8 18.8 %shard_map.57 = f32[32,128]{1,0:T(8,128)S(1)} custom-call(s32[3,63]{1,0:T(4,128)S(1)} %pad_add_fusion.1.items, s32[1]{0:T(128)} %bitcast.4.place, bf16[2,4,32,2048]{3,2,1,0:T(8,128)(2,1)} %bitcast.29, bf16[3,32,2048]{2,1,0:T(8,128)(2,1)S(1)} %get-tuple-element.27.refs_0_, bf16[3,32,2048]{2,1,0:T(8,128)(2,1)S(1)} %collective-permute-done.6.refs_1_, ...), custom_call_target="tpu_custom_call" | custom-call | flops 12884901888 | bytes 16777216 | tf_op jit(solution)/shard_map/pallas_call | solution.py:148
  122.6 19.0 %shard_map.56 = f32[32,128]{1,0:T(8,128)S(1)} custom-call(s32[3,63]{1,0:T(4,128)S(1)} %pad_add_fusion.1.items, s32[1]{0:T(128)} %bitcast.4.place, bf16[2,4,32,2048]{3,2,1,0:T(8,128)(2,1)} %bitcast.30, bf16[3,32,2048]{2,1,0:T(8,128)(2,1)S(1)} %get-tuple-element.27.refs_0_, bf16[3,32,2048]{2,1,0:T(8,128)(2,1)S(1)} %collective-permute-done.6.refs_1_, ...), custom_call_target="tpu_custom_call" | custom-call | flops 12884901888 | bytes 16777216 | tf_op jit(solution)/shard_map/pallas_call | solution.py:148
  141.7 11.3 %all_to_all.5 = f32[16,4,256]{2,1,0:T(4,128)S(1)} all-to-all(f32[16,4,256]{2,1,0:T(4,128)S(1)} %maximum_bitcast_fusion), channel_id=1, replica_groups=mesh['groups'=2,'wide'=4,'narrow'=4] {'wide','narrow'}, dimensions={0} | all-to-all | bytes 131072 | tf_op jit(solution)/shard_map/all_to_all | solution.py:226
  153.0 0.6 broadcast_multiply_fusion
  (53 shorter events, 1.3 us)
Async XLA Ops:
  6.5 56.6 %all-gather.5.cloned.1.call-start = ((), (), s32[]{:S(2)}) async-start(), calls=%async_computation.1 | async-start | bytes 1310720 | tf_op jit(solution)/shard_map/all_gather | solution.py:198
  6.5 7.0 %slice-start = ((bf16[4,32,4096]{2,1,0:T(8,128)(2,1)}), bf16[1,32,4096]{2,1,0:T(8,128)(2,1)S(1)}, s32[]{:S(2)}) async-start(bf16[4,32,4096]{2,1,0:T(8,128)(2,1)} %param.6), calls=%async_computation.5 | async-start | bytes 524288 | tf_op jit(solution)/shard_map/slice | solution.py:203
  6.5 12.4 %copy-start.2 = (s32[4096]{0:T(1024)S(1)}, s32[4096]{0:T(1024)}, u32[]{:S(2)}) copy-start(s32[4096]{0:T(1024)} %param.9) | copy-start | bytes 49156
  6.5 12.4 %copy-start.3 = (s32[4096]{0:T(1024)S(1)}, s32[4096]{0:T(1024)}, u32[]{:S(2)}) copy-start(s32[4096]{0:T(1024)} %param.8) | copy-start | bytes 49156
  9.5 22.4 %collective-permute-start = (u16[128,2048]{1,0:T(8,128)(2,1)}, u16[128,2048]{1,0:T(8,128)(2,1)S(1)}, u32[]{:S(2)}, u32[]{:S(2)}) collective-permute-start(u16[128,2048]{1,0:T(8,128)(2,1)} %get-tuple-element.23), channel_id=1, source_target_pairs={{0,1},{1,0},{2,3},{3,2},{4,5},{5,4},{6,7},{7,6},{8,9},{9,8},{10,11... | collective-permute-start | bytes 1572872 | tf_op jit(solution)/shard_map/ppermute | solution.py:192
  13.5 17.7 %collective-permute-start.1 = (bf16[32,2048]{1,0:T(8,128)(2,1)S(1)}, bf16[32,2048]{1,0:T(8,128)(2,1)S(1)}, u32[]{:S(2)}, u32[]{:S(2)}) collective-permute-start(bf16[32,2048]{1,0:T(8,128)(2,1)S(1)} %get-tuple-element.29), channel_id=1, source_target_pairs={{0,1},{1,0},{2,3},{3,2},{4,5},{5,4},{6,7},{7,6},{8,9},{9,8},{10,11... | collective-permute-start | bytes 393224 | tf_op jit(solution)/shard_map/ppermute | solution.py:192
  13.6 18.4 %slice-start.1 = ((bf16[4,32,4096]{2,1,0:T(8,128)(2,1)}), bf16[3,32,4096]{2,1,0:T(8,128)(2,1)S(1)}, s32[]{:S(2)}) async-start(bf16[4,32,4096]{2,1,0:T(8,128)(2,1)} %param.6), calls=%async_computation.6 | async-start | bytes 1572864 | tf_op jit(solution)/shard_map/slice | solution.py:207
  14.4 47.3 %collective-permute-start.2 = (bf16[1,32,2048]{2,1,0:T(8,128)(2,1)}, bf16[1,32,2048]{2,1,0:T(8,128)(2,1)S(1)}, u32[]{:S(2)}, u32[]{:S(2)}) collective-permute-start(bf16[1,32,2048]{2,1,0:T(8,128)(2,1)} %get-tuple-element.38), channel_id=1, source_target_pairs={{0,1},{1,0},{2,3},{3,2},{4,5},{5,4},{6,7},{7,6},{8,9},{9,8},{10,11... | collective-permute-start | bytes 393224 | tf_op jit(solution)/shard_map/ppermute | solution.py:192
  16.3 46.8 %collective-permute-start.3 = (bf16[1,32,2048]{2,1,0:T(8,128)(2,1)}, bf16[1,32,2048]{2,1,0:T(8,128)(2,1)S(1)}, u32[]{:S(2)}, u32[]{:S(2)}) collective-permute-start(bf16[1,32,2048]{2,1,0:T(8,128)(2,1)} %get-tuple-element.37), channel_id=1, source_target_pairs={{0,2},{1,3},{2,0},{3,1},{4,6},{5,7},{6,4},{7,5},{8,10},{9,11},{10,... | collective-permute-start | bytes 393224 | tf_op jit(solution)/shard_map/ppermute | solution.py:192
  18.9 44.3 %collective-permute-start.4 = (bf16[1,32,2048]{2,1,0:T(8,128)(2,1)S(1)}, bf16[1,32,2048]{2,1,0:T(8,128)(2,1)S(1)}, u32[]{:S(2)}, u32[]{:S(2)}) collective-permute-start(bf16[1,32,2048]{2,1,0:T(8,128)(2,1)S(1)} %get-tuple-element.36), channel_id=1, source_target_pairs={{0,3},{1,2},{2,1},{3,0},{4,7},{5,6},{6,5},{7,4},{8,11},{9,10},{10,... | collective-permute-start | bytes 393224 | tf_op jit(solution)/shard_map/ppermute | solution.py:192
  31.9 52.9 %all-gather.11.cloned.1.call-start = ((), (), s32[]{:S(2)}) async-start(), calls=%async_computation.4 | async-start | bytes 1310720 | tf_op jit(solution)/shard_map/all_gather | solution.py:198
  31.9 14.2 %collective-permute-start.5 = (bf16[3,32,2048]{2,1,0:T(8,128)(2,1)S(1)}, bf16[3,32,2048]{2,1,0:T(8,128)(2,1)S(1)}, u32[]{:S(2)}, u32[]{:S(2)}) collective-permute-start(bf16[3,32,2048]{2,1,0:T(8,128)(2,1)S(1)} %slice.34), channel_id=1, source_target_pairs={{0,1},{1,0},{2,3},{3,2},{4,5},{5,4},{6,7},{7,6},{8,9},{9,8},{10,11... | collective-permute-start | bytes 1179656 | tf_op jit(solution)/shard_map/ppermute | solution.py:192
  33.1 51.7 %collective-permute-start.6 = (bf16[3,32,2048]{2,1,0:T(8,128)(2,1)}, bf16[3,32,2048]{2,1,0:T(8,128)(2,1)S(1)}, u32[]{:S(2)}, u32[]{:S(2)}) collective-permute-start(bf16[3,32,2048]{2,1,0:T(8,128)(2,1)} %get-tuple-element.26), channel_id=1, source_target_pairs={{0,1},{1,0},{2,3},{3,2},{4,5},{5,4},{6,7},{7,6},{8,9},{9,8},{10,11... | collective-permute-start | bytes 1179656 | tf_op jit(solution)/shard_map/ppermute | solution.py:192
  46.1 38.6 %collective-permute-start.7 = (bf16[3,32,2048]{2,1,0:T(8,128)(2,1)}, bf16[3,32,2048]{2,1,0:T(8,128)(2,1)S(1)}, u32[]{:S(2)}, u32[]{:S(2)}) collective-permute-start(bf16[3,32,2048]{2,1,0:T(8,128)(2,1)} %get-tuple-element.25), channel_id=1, source_target_pairs={{0,2},{1,3},{2,0},{3,1},{4,6},{5,7},{6,4},{7,5},{8,10},{9,11},{10,... | collective-permute-start | bytes 1179656 | tf_op jit(solution)/shard_map/ppermute | solution.py:192
  49.0 54.8 %all-gather.9.cloned.1.call-start = ((), (), s32[]{:S(2)}) async-start(), calls=%async_computation.3 | async-start | bytes 1310720 | tf_op jit(solution)/shard_map/all_gather | solution.py:198
  54.6 68.0 %all-gather.7.cloned.1.call-start = ((), (), s32[]{:S(2)}) async-start(), calls=%async_computation.2 | async-start | bytes 1310720 | tf_op jit(solution)/shard_map/all_gather | solution.py:198
  57.7 4.0 %copy-start.1 = (bf16[3,32,2048]{2,1,0:T(8,128)(2,1)S(1)}, bf16[3,32,2048]{2,1,0:T(8,128)(2,1)}, u32[]{:S(2)}) copy-start(bf16[3,32,2048]{2,1,0:T(8,128)(2,1)} %get-tuple-element.24) | copy-start | bytes 1179652
  61.7 23.0 %collective-permute-start.8 = (bf16[3,32,2048]{2,1,0:T(8,128)(2,1)S(1)}, bf16[3,32,2048]{2,1,0:T(8,128)(2,1)S(1)}, u32[]{:S(2)}, u32[]{:S(2)}) collective-permute-start(bf16[3,32,2048]{2,1,0:T(8,128)(2,1)S(1)} %copy-done.1), channel_id=1, source_target_pairs={{0,3},{1,2},{2,1},{3,0},{4,7},{5,6},{6,5},{7,4},{8,11},{9,10},{10,... | collective-permute-start | bytes 1179656 | tf_op jit(solution)/shard_map/ppermute | solution.py:192
  63.2 3.2 %copy-start = (bf16[2,128,2048]{2,1,0:T(8,128)(2,1)S(1)}, bf16[2,128,2048]{2,1,0:T(8,128)(2,1)}, u32[]{:S(2)}) copy-start(bf16[2,128,2048]{2,1,0:T(8,128)(2,1)} %all-gather.5.cloned.1.call-done) | copy-start | bytes 3145732
Sparse Core Ops, SparseCore 0:
  32.0 18.5 all-gather.4
  52.1 16.6 all-gather.10
  70.4 16.7 all-gather.8
  88.6 16.6 all-gather.6

commit v2 on v1

--- a/solution.py
+++ b/solution.py
@@ -35,33 +35,71 @@
     return lax.sort((key, lax.iota(jnp.int32, key.shape[0])), num_keys=1)
 
 
-def plan(key, order, base, na, nh):
+def factor_body(na, tops, base, key_ref, order_ref, pick, flip, lane, low, high):
+    d = lax.broadcasted_iota(jnp.int32, (TILE, LANES), 1)
+    low_bits = LOW.bit_length() - 1
+    na_bits = na.bit_length() - 1
+    place = base[0] ^ ((d >> low_bits) & (na - 1) | d >> (low_bits + na_bits) << ROW_HIGH)
+    coarse = lax.broadcasted_iota(jnp.int32, (high.shape[0], LANES), 0)
+
+    def down(ref, t):
+        return jnp.broadcast_to(ref[pl.ds(t, 1), :], (TILE, LANES)).T
+
+    def sign(odd):
+        return (1 - 2 * (odd & 1)).astype(jnp.float32)
+
+    def tile(t, carry):
+        at_t = pl.ds(pl.multiple_of(t * TILE, TILE), TILE)
+        key = down(key_ref, t)
+        col = key & (FF - 1)
+        row_low = key >> (COL_BITS + ROW_HIGH)
+        code = (key >> COL_BITS) & (D // BLK - 1) | col // BLK << ROW_HIGH
+        odd = code & place
+        for b in (8, 4, 2, 1):
+            odd = odd ^ odd >> b
+        pick[at_t, :] = jnp.where((row_low ^ d) & (LOW - 1) == 0, sign(odd), 0.0).astype(jnp.bfloat16)
+        for b in range(tops):
+            bit = LANES.bit_length() - 1 + b - low_bits
+            bit = bit if bit < na_bits else bit - na_bits + ROW_HIGH
+            flip[b, at_t, :] = sign(code >> bit).astype(jnp.bfloat16)
+        odd = col & d
+        for b in (4, 2, 1):
+            odd = odd ^ odd >> b
+        lane[at_t, :LANES] = sign(odd).astype(jnp.bfloat16)
+        lane[at_t, LANES:] = sign(odd ^ col >> 7).astype(jnp.bfloat16)
+        low[at_t, :] = jnp.where((down(order_ref, t) ^ d) & (LANES - 1) == 0, 1.0, 0.0).astype(jnp.bfloat16)
+        high[:, at_t] = jnp.where(order_ref[pl.ds(t, 1), :] >> 7 == coarse, 1.0, 0.0).astype(jnp.bfloat16)
+        return carry
+
+    lax.fori_loop(0, key_ref.shape[0], tile, 0, unroll=4)
+
+
+def slot_factors(key, order, base, na, nh):
     k = key.shape[0]
-    col = key & (FF - 1)
-    row_low = key >> (COL_BITS + ROW_HIGH)
-    group = row_low // LOW
-    code = (key >> COL_BITS) & (D // BLK - 1) | (col // BLK) << ROW_HIGH
-    d = jnp.arange(LANES, dtype=jnp.int32)
-
-    def bits_of(d):
-        return (d // LOW) % na | d // (LOW * na) << ROW_HIGH
-
-    hit = (row_low & (LOW - 1))[:, None] == (d % LOW)[None, :]
-    pick = jnp.where(hit, parity_sign(code[:, None], (base ^ bits_of(d))[None, :]), 0).astype(jnp.bfloat16)
     tops = (na * nh * LOW // LANES).bit_length() - 1
-    top = bits_of(LANES << jnp.arange(max(tops, 1), dtype=jnp.int32))
-    flip = jnp.broadcast_to(parity_sign(code[None, :], top[:, None])[:, :, None], (max(tops, 1), k, LANES))
-    lane = parity_sign((col & (BLK - 1))[:, None], jnp.arange(BLK, dtype=jnp.int32)[None, :])
-    tiles = k // TILE
-    low_hot = ((order % LANES)[:, None] == d[None, :]).astype(jnp.bfloat16)
-    high = jnp.arange(k // LANES, dtype=jnp.int32)
-    high_hot = ((order // LANES)[None, :] == high[:, None]).astype(jnp.bfloat16)
-    ends = jnp.sum((group[None, :] <= jnp.arange(GROUPS, dtype=jnp.int32)[:, None]).astype(jnp.int32), axis=1)
-    cuts = jnp.sort(jnp.concatenate([jnp.arange(tiles, dtype=jnp.int32) * TILE, ends[:-1]]))
-    item_tile = jnp.minimum(cuts // TILE, tiles - 1)
-    item_group = jnp.minimum(jnp.sum((ends[None, :] <= cuts[:, None]).astype(jnp.int32), axis=1), GROUPS - 1)
-    items = jnp.stack([item_tile, item_group, cuts - item_tile * TILE])
-    return items, pick, flip, lane, low_hot, high_hot
+    tiles = 8
+    parts = k // TILE // tiles
+    some = lambda *shape: jax.ShapeDtypeStruct(shape, jnp.bfloat16)
+    rows = lambda width: pl.BlockSpec((k // parts, width), lambda i, *s: (i, 0))
+    ids = pl.BlockSpec((tiles, LANES), lambda i, *s: (i, 0))
+    return pl.pallas_call(
+        functools.partial(factor_body, na, tops),
+        out_shape=[some(k, LANES), some(max(tops, 1), k, LANES), some(k, BLK), some(k, LANES), some(k // LANES, k)],
+        grid_spec=pltpu.PrefetchScalarGridSpec(
+            num_scalar_prefetch=1,
+            grid=(parts,),
+            in_specs=[ids, ids],
+            out_specs=[
+                rows(LANES),
+                pl.BlockSpec((max(tops, 1), k // parts, LANES), lambda i, *s: (0, i, 0)),
+                rows(BLK),
+                rows(LANES),
+                pl.BlockSpec((k // LANES, k // parts), lambda i, *s: (0, i)),
+            ],
+        ),
+        compiler_params=pltpu.CompilerParams(vmem_limit_bytes=60 << 20),
+        cost_estimate=pl.CostEstimate(flops=80 * k * LANES, bytes_accessed=2 * k * LANES * 8, transcendentals=0),
+    )(base, key.reshape(k // LANES, LANES), order.reshape(k // LANES, LANES))
 
 
 def halve(x):
@@ -69,7 +107,7 @@
     return coarse, (x - coarse.astype(jnp.float32)).astype(jnp.bfloat16)
 
 
-def body(parts, na, nc, steps, tops, unroll, items, place, a_ref, *refs):
+def body(parts, na, nc, steps, tops, unroll, ends, place, a_ref, *refs):
     g_refs = refs[:parts]
     words_ref, h_ref, pick_hbm, flip_hbm, lane_hbm, low_hbm, high_ref, out_ref, at, w, pick, flip, lane, low, part, spread, sems = refs[parts:]
     step = pl.program_id(0)
@@ -109,18 +147,25 @@
             c.wait()
         slot = lax.broadcasted_iota(jnp.int32, (TILE, LANES), 0)
 
+        tiles = pick.shape[0] // TILE
+
         def item(i, carry):
-            t, g = items[0, i], items[1, i]
+            t, g, start = carry
             at_t = pl.ds(pl.multiple_of(t * TILE, TILE), TILE)
             signs = [pick[at_t, :]]
             for b in range(tops):
                 signs += [s * flip[b, at_t, :] for s in signs]
             mixed = jnp.dot(jnp.concatenate(signs, axis=1), w[g], preferred_element_type=jnp.float32)
             mixed = mixed * lane[at_t, :].astype(jnp.float32)
-            part[at_t, :] = jnp.where(slot >= items[2, i], mixed[:, :LANES] + mixed[:, LANES:], part[at_t, :])
-            return carry
-
-        lax.fori_loop(0, items.shape[1], item, 0, unroll=unroll)
+            part[at_t, :] = jnp.where(slot >= start - t * TILE, mixed[:, :LANES] + mixed[:, LANES:], part[at_t, :])
+            stop, last = ends[g], (t + 1) * TILE
+            onward = (g < GROUPS - 1) & (stop <= last)
+            g = jnp.where(onward, g + 1, g)
+            t = jnp.minimum(jnp.where(onward, t, t + 1), tiles - 1)
+            return t, g, jnp.where(onward, stop, last)
+
+        zero = jnp.int32(0)
+        lax.fori_loop(0, tiles + GROUPS - 1, item, (zero, zero, zero), unroll=unroll)
         ones = jnp.ones((LANES, LANES), jnp.bfloat16)
 
         def back(t, carry):
@@ -134,8 +179,8 @@
         out_ref[...] = sum(jnp.dot(high_ref[...], spread[i], preferred_element_type=jnp.float32) for i in (0, 1))
 
 
-def sketch_terms(items, place, a, example, g_parts, words, h, pick, flip, lane, low_hot, high_hot):
-    blocks, parts, few, span = a.shape
+def sketch_terms(ends, place, panel, example, g_parts, words, h, pick, flip, lane, low_hot, high_hot):
+    blocks, parts, few, span = panel.shape
     rows, cols = 16 * words.shape[0], words.shape[1]
     wide = min(cols, WIDE)
     steps = cols // wide
@@ -144,21 +189,21 @@
     depth = na * nc * steps * LOW
     tops = (depth // LANES).bit_length() - 1
     whole = lambda *shape: pl.BlockSpec(shape, lambda j, *s: (0,) * len(shape))
-    hbm = pl.BlockSpec(memory_space=pl.ANY)
+    hbm = pl.BlockSpec(memory_space=pltpu.HBM)
     return pl.pallas_call(
         functools.partial(body, parts, na, nc, steps, tops, 21),
         out_shape=jax.ShapeDtypeStruct((k // LANES, LANES), jnp.float32),
         grid_spec=pltpu.PrefetchScalarGridSpec(
             num_scalar_prefetch=2,
             grid=(steps,),
-            in_specs=[whole(*a.shape)]
+            in_specs=[whole(blocks, parts, few, span)]
             + [pl.BlockSpec((None, few, wide), lambda j, *s: (example, 0, j))] * parts
             + [pl.BlockSpec((rows // 16, wide), lambda j, *s: (0, j)), whole(BLK, BLK)]
             + [hbm] * 4
             + [whole(*high_hot.shape)],
             out_specs=whole(k // LANES, LANES),
             scratch_shapes=[
-                pltpu.VMEM((rows, a.shape[1] * few), jnp.bfloat16),
+                pltpu.VMEM((rows, parts * few), jnp.bfloat16),
                 pltpu.VMEM((GROUPS, depth, BLK), jnp.bfloat16),
                 pltpu.VMEM(pick.shape, jnp.bfloat16),
                 pltpu.VMEM(flip.shape, jnp.bfloat16),
@@ -173,7 +218,7 @@
         cost_estimate=pl.CostEstimate(
             flops=2 * rows * wide * steps * 3 * BLK, bytes_accessed=2 * rows * wide * steps, transcendentals=0
         ),
-    )(items, place, a, *g_parts, words, h, pick, flip, lane, low_hot, high_hot)
+    )(ends, place, panel, *g_parts, words, h, pick, flip, lane, low_hot, high_hot)
 
 
 def local(sizes, share, activations, out_grads, sign_bits, kept_row, kept_col):
@@ -194,33 +239,41 @@
     def columns(x, s):
         return lax.dynamic_slice_in_dim(x, ((n ^ s) % share) * col_len, col_len, x.ndim - 1)
 
-    def panel(shards):
-        return lax.all_gather(jnp.stack(shards), "wide", axis=1, tiled=True)
-
-    near = [activations[0]] + [swap(activations[0], s) for s in range(1, share)]
-    panels = [panel(near)]
+    def spread(x):
+        return [x] + [swap(x, s) for s in range(1, share)]
+
+    def panel(rows):
+        return lax.all_gather(jnp.stack(rows), "wide", axis=1, tiled=True).reshape(share, narrow_size, few, row_len)
+
+    near = spread(activations[:2])
     words = [columns(sign_bits, 0)] + [swap(columns(sign_bits, s).astype(jnp.uint16), s) for s in range(1, share)]
-    outs = out_grads[:1]
-    grads = [(0, [columns(outs, 0)] + [swap(columns(outs, s), s) for s in range(1, narrow_size)])]
+    outs = out_grads[:2]
+    outs = [columns(outs, 0)] + [swap(columns(outs, s), s) for s in range(1, narrow_size)]
+    grads = [(e, outs) for e in range(2)]
     key, order = in_groups(kept_row, kept_col)
-    acts, outs, key, order, *_ = lax.optimization_barrier(
-        (activations[1:], out_grads[1:], key, order, words[-1], near[-1])
-    )
+    key, order, near = lax.optimization_barrier((key, order, near))
+    first = near[-1]
+    outs, acts, *_ = lax.optimization_barrier((out_grads[2:], activations[2:], words[-1], first))
     words = jnp.concatenate([x.astype(jnp.int32) for x in words])
-    others = [acts] + [swap(acts, s) for s in range(1, share)]
     rest = [columns(outs, 0)] + [swap(columns(outs, s), s) for s in range(1, narrow_size)]
-    for e in range(count - 1):
-        panels.append(panel([x[e] for x in others]))
-        grads.append((e, rest))
+    grads += [(e, rest) for e in range(count - 2)]
+    panels = [panel([x[e] for x in near]) for e in range(2)]
+    far = spread(acts)
     base = n * (row_len // BLK) | ((wide_idx * share + n % share) * nh) << ROW_HIGH
-    factors = plan(key, order, base, na, nh)
+    factors = slot_factors(key, order, jnp.full((1,), base, jnp.int32), na, nh)
+    groups = jnp.arange(GROUPS, dtype=jnp.int32)
+    ends = jnp.sum(((kept_row & (BLK - 1)) // LOW <= groups[:, None]).astype(jnp.int32), axis=1)
     index = jnp.arange(BLK, dtype=jnp.int32)
     h = parity_sign(index[:, None], index[None, :])
     place = jnp.full((1,), n, jnp.int32)
     terms = []
     for e in range(count):
-        a = panels[e].reshape(share, narrow_size, few, row_len)
-        terms.append(sketch_terms(factors[0], place, a, *grads[e], words, h, *factors[1:]))
+        if e == 1:
+            far, _ = lax.optimization_barrier((far, terms[0]))
+            panels += [panel([x[i] for x in far]) for i in range(count - 2)]
+        if e:
+            ends, _ = lax.optimization_barrier((ends, terms[-1]))
+        terms.append(sketch_terms(ends, place, panels[e], *grads[e], words, h, *factors))
     owners = wide_size * narrow_size
     send = jnp.stack(terms).reshape(count, owners, k // owners).transpose(1, 0, 2)
     got = lax.all_to_all(send, ("wide", "narrow"), 0, 0, tiled=True)

time: 161 us -> 152 us (0.944)
  other arithmetic: 25.9 us -> 16.2 us
  Pallas kernels: 75.1 us -> 83.6 us
  waiting for transfers between devices: 13.8 us -> 7.67 us
  local copies, waits for them, and re-layouts: 7.04 us -> 5.08 us
    pallas_call x0 -> x1, Pallas kernels: none -> 8.31 us  [slot_factors(): pl.pallas_call(functools.partial(factor_body, na, tops), out_shape=[some(...]
    ppermute x9, waiting for transfers between devices: 13.7 us -> 7.54 us  [swap(): return lax.ppermute(x, 'narrow', [(j, j ^ s) for j in range(narrow_size)])]
    convert_element_type x3 -> x1, other arithmetic: 3.5 us -> 0.12 us  [parity_sign(): return (1 - 2 * (folded & 1)).astype(jnp.bfloat16)]
    broadcast_in_dim x1 -> x0, local copies, waits for them, and re-layouts: 3.18 us -> none  [plan(): jnp.broadcast_to(parity_sign(code[None, :], top[:, None])[:, :, None], (m...]
    convert_element_type x2 -> x0, other arithmetic: 2.79 us -> none  [the longest x1 2.74 us: plan(): low_hot = ((order % LANES)[:, None] == d[None, :]).astype(jnp.bfloat16)]
    select_n x3 -> x0, other arithmetic: 2.57 us -> none  [the longest x1 2.52 us: plan(): jnp.where(hit, parity_sign(code[:, None], (base ^ bits_of(d))[None, :]), 0)]
    sort x1 -> x0, other arithmetic: 2.05 us -> none  [plan(): jnp.sort(jnp.concatenate([jnp.arange(tiles, dtype=jnp.int32) * TILE, ends...]
    slice x8 -> x5, local copies, waits for them, and re-layouts: 2.01 us -> 3.38 us  [the longest x1 1.27 us: local(): out_grads[2:]]
  transfers between devices with their start and end apart: 13 -> 13, of which waited for: 2 -> 1; matrix products, arithmetic and copies ran while one was open for 18% -> 13% of each run, Pallas kernels for 35% -> 43%
where the time goes in v2:
time: 152 us; the launch traced here: 151 us
  Pallas kernels  83.6 us (55%)
  other arithmetic  16.2 us (11%)
  starting transfers between devices  13.4 us (9%)
  between operations  13.3 us (9%)
  blocking collectives  12.2 us (8%)
  waiting for transfers between devices  7.67 us (5%)
  local copies, waits for them, and re-layouts  5.08 us (3%)
    pallas_call x4, Pallas kernels, sketch_terms(): pl.pallas_call(functools.partial(body, parts, na, nc, steps, tops, 21), o...  75.3 us
    ppermute x9, starting transfers between devices, swap(): return lax.ppermute(x, 'narrow', [(j, j ^ s) for j in range(narrow_size)])  13 us
    all_to_all x1, blocking collectives, local(): got = lax.all_to_all(send, ('wide', 'narrow'), 0, 0, tiled=True)  12.2 us
    pallas_call x1, Pallas kernels, slot_factors(): pl.pallas_call(functools.partial(factor_body, na, tops), out_shape=[some(...  8.31 us
    ppermute x9, waiting for transfers between devices, swap(): return lax.ppermute(x, 'narrow', [(j, j ^ s) for j in range(narrow_size)])  7.54 us
    sort x1, other arithmetic, in_groups(): return lax.sort((key, lax.iota(jnp.int32, key.shape[0])), num_keys=1)  5.78 us
  transfers between devices with their start and end apart: 13, of which 1 were waited for; matrix products, arithmetic and copies ran while one was open for 13% of the time, Pallas kernels for 43%

profile of v2, /device:TPU:0, one launch (start us, length us, event | category | flops | bytes accessed | tf_op | source)
XLA Modules:
  0.0 151.4 jit_solution(11563997045800428976)
XLA Ops:
  6.5 1.1 fusion.12
  7.6 3.1 %collective-permute-start = (bf16[2,32,2048]{2,1,0:T(8,128)(2,1)S(1)}, bf16[2,32,2048]{2,1,0:T(8,128)(2,1)S(1)}, u32[]{:S(2)}, u32[]{:S(2)}) collective-permute-start(bf16[2,32,2048]{2,1,0:T(8,128)(2,1)S(1)} %get-tuple-element.25), channel_id=1, source_target_pairs={{0,1},{1,0},{2,3},{3,2},{4,5},{5,4},{6,7},{7,6},{8,9},{9,8},{10,11... | collective-permute-start | bytes 786440 | tf_op jit(solution)/shard_map/ppermute | solution.py:237
  10.7 2.5 %constant_dynamic-slice_fusion.4 = (s32[128,2048]{1,0:T(8,128)S(1)}, u16[128,2048]{1,0:T(8,128)(2,1)}) fusion(s32[128,4096]{1,0:T(8,128)} %param.7, s32[]{:T(128)S(6)} %select_n.62, s32[]{:T(128)S(6)} %select_n.64), kind=kLoop, calls=%fused_computation.38 | loop fusion | flops 262144 | bytes 3670024 | tf_op jit(solution)/shard_map/dynamic_slice | solution.py:240
  13.3 0.6 fusion.8
  13.9 5.8 %sort.15 = (s32[4096]{0:T(1024)}, s32[4096]{0:T(1024)}) sort(s32[4096]{0:T(1024)S(1)} %get-tuple-element.63, s32[4096]{0:T(1024)S(1)} %iota.14), dimensions={0}, to_apply=%region_1.2 | sort | flops 49152 | bytes 65536 | tf_op jit(solution)/shard_map/sort | solution.py:35
  19.7 0.7 pad_maximum_fusion
  20.5 1.3 fusion.11
  21.8 0.9 constant_dynamic-slice_fusion.5
  22.7 2.0 %collective-permute-start.1 = (bf16[2,32,2048]{2,1,0:T(8,128)(2,1)}, bf16[2,32,2048]{2,1,0:T(8,128)(2,1)S(1)}, u32[]{:S(2)}, u32[]{:S(2)}) collective-permute-start(bf16[2,32,2048]{2,1,0:T(8,128)(2,1)} %get-tuple-element.53), channel_id=1, source_target_pairs={{0,1},{1,0},{2,3},{3,2},{4,5},{5,4},{6,7},{7,6},{8,9},{9,8},{10,11... | collective-permute-start | bytes 786440 | tf_op jit(solution)/shard_map/ppermute | solution.py:237
  24.7 2.6 %collective-permute-start.2 = (bf16[2,32,2048]{2,1,0:T(8,128)(2,1)}, bf16[2,32,2048]{2,1,0:T(8,128)(2,1)S(1)}, u32[]{:S(2)}, u32[]{:S(2)}) collective-permute-start(bf16[2,32,2048]{2,1,0:T(8,128)(2,1)} %get-tuple-element.52), channel_id=1, source_target_pairs={{0,2},{1,3},{2,0},{3,1},{4,6},{5,7},{6,4},{7,5},{8,10},{9,11},{10,... | collective-permute-start | bytes 786440 | tf_op jit(solution)/shard_map/ppermute | solution.py:237
  27.3 0.1 fusion.3.refs_5_
  27.4 0.9 convert_reduce_fusion.ends
  28.3 0.8 pad_maximum_fusion.1
  29.1 8.3 %shard_map.55 = (bf16[4096,128]{1,0:T(8,128)(2,1)}, bf16[3,4096,128]{2,1,0:T(8,128)(2,1)}, bf16[4096,256]{1,0:T(8,128)(2,1)}, bf16[4096,128]{1,0:T(8,128)(2,1)}, bf16[32,4096]{1,0:T(8,128)(2,1)}) custom-call(s32[1]{0:T(128)} %bitcast.2.base, s32[32,128]{1,0:T(8,128)} %bitcast.22, s32[32,128]{1,0:T(8,128)} %bitcast.23), custom_call_target="tpu_custom_call" | custom-call | flops 41943040 | bytes 8388608 | tf_op jit(solution)/shard_map/pallas_call | solution.py:85
  37.4 1.0 collective-permute-start.5
  38.4 1.1 convert_element_type.20
  39.5 1.5 pad_add_fusion.refs_4_
  41.0 7.5 %collective-permute-done.3.refs_3_ = bf16[2,32,2048]{2,1,0:T(8,128)(2,1)S(1)} collective-permute-done((bf16[2,32,2048]{2,1,0:T(8,128)(2,1)S(1)}, bf16[2,32,2048]{2,1,0:T(8,128)(2,1)S(1)}, u32[]{:S(2)}, u32[]{:S(2)}) %collective-permute-start.3) | collective-permute-done | bytes 262176 | tf_op jit(solution)/shard_map/ppermute | solution.py:237
  48.6 18.7 %shard_map.56 = f32[32,128]{1,0:T(8,128)S(1)} custom-call(s32[32]{0:T(128)S(1)} %convert_reduce_fusion.ends, s32[1]{0:T(128)} %bitcast.place, bf16[2,4,32,2048]{3,2,1,0:T(8,128)(2,1)} %bitcast.19, bf16[2,32,2048]{2,1,0:T(8,128)(2,1)S(1)} %get-tuple-element.54.refs_0_, bf16[2,32,2048]{2,1,0:T(8,128)(2,1)S(1)} %collective-permute-done.1.refs_1_, ...), custom_call_target="tpu_custom_call" | custom-call | flops 12884901888 | bytes 16777216 | tf_op jit(solution)/shard_map/pallas_call | solution.py:193
  67.3 1.0 fusion.14
  68.3 0.7 pad_maximum_fusion.2
  69.1 0.2 all-gather.11.cloned.1.call-start
  69.3 0.8 constant_dynamic-slice_fusion
  70.1 1.9 %collective-permute-start.6 = (bf16[2,32,2048]{2,1,0:T(8,128)(2,1)}, bf16[2,32,2048]{2,1,0:T(8,128)(2,1)S(1)}, u32[]{:S(2)}, u32[]{:S(2)}) collective-permute-start(bf16[2,32,2048]{2,1,0:T(8,128)(2,1)} %get-tuple-element.47), channel_id=1, source_target_pairs={{0,1},{1,0},{2,3},{3,2},{4,5},{5,4},{6,7},{7,6},{8,9},{9,8},{10,11... | collective-permute-start | bytes 786440 | tf_op jit(solution)/shard_map/ppermute | solution.py:237
  72.0 1.0 collective-permute-start.7
  73.0 1.5 collective-permute-start.8
  74.5 0.8 pad_maximum_fusion.3
  75.3 18.8 %shard_map.57 = f32[32,128]{1,0:T(8,128)S(1)} custom-call(s32[32]{0:T(128)S(1)} %convert_reduce_fusion.ends, s32[1]{0:T(128)} %bitcast.place, bf16[2,4,32,2048]{3,2,1,0:T(8,128)(2,1)} %bitcast.18, bf16[2,32,2048]{2,1,0:T(8,128)(2,1)S(1)} %get-tuple-element.54.refs_0_, bf16[2,32,2048]{2,1,0:T(8,128)(2,1)S(1)} %collective-permute-done.1.refs_1_, ...), custom_call_target="tpu_custom_call" | custom-call | flops 12884901888 | bytes 16777216 | tf_op jit(solution)/shard_map/pallas_call | solution.py:193
  94.1 18.9 %shard_map.58 = f32[32,128]{1,0:T(8,128)S(1)} custom-call(s32[32]{0:T(128)S(1)} %convert_reduce_fusion.ends, s32[1]{0:T(128)} %bitcast.place, bf16[2,4,32,2048]{3,2,1,0:T(8,128)(2,1)} %bitcast.20, bf16[2,32,2048]{2,1,0:T(8,128)(2,1)S(1)} %get-tuple-element.48.refs_0_, bf16[2,32,2048]{2,1,0:T(8,128)(2,1)S(1)} %collective-permute-done.6.refs_1_, ...), custom_call_target="tpu_custom_call" | custom-call | flops 12884901888 | bytes 16777216 | tf_op jit(solution)/shard_map/pallas_call | solution.py:193
  113.0 18.9 %shard_map.59 = f32[32,128]{1,0:T(8,128)S(1)} custom-call(s32[32]{0:T(128)S(1)} %convert_reduce_fusion.ends, s32[1]{0:T(128)} %bitcast.place, bf16[2,4,32,2048]{3,2,1,0:T(8,128)(2,1)} %bitcast.21, bf16[2,32,2048]{2,1,0:T(8,128)(2,1)S(1)} %get-tuple-element.48.refs_0_, bf16[2,32,2048]{2,1,0:T(8,128)(2,1)S(1)} %collective-permute-done.6.refs_1_, ...), custom_call_target="tpu_custom_call" | custom-call | flops 12884901888 | bytes 16777216 | tf_op jit(solution)/shard_map/pallas_call | solution.py:193
  132.1 12.2 %all_to_all.5 = f32[16,4,256]{2,1,0:T(4,128)S(1)} all-to-all(f32[16,4,256]{2,1,0:T(4,128)S(1)} %maximum_bitcast_fusion), channel_id=1, replica_groups=mesh['groups'=2,'wide'=4,'narrow'=4] {'wide','narrow'}, dimensions={0} | all-to-all | bytes 131072 | tf_op jit(solution)/shard_map/all_to_all | solution.py:279
  144.3 0.6 broadcast_multiply_fusion
  (32 shorter events, 0.5 us)
Async XLA Ops:
  6.5 42.0 %all-gather.5.cloned.1.call-start = ((), (), s32[]{:S(2)}) async-start(), calls=%async_computation.1 | async-start | bytes 1310720 | tf_op jit(solution)/shard_map/all_gather | solution.py:246
  7.6 5.7 %copy-start.1 = (s32[4096]{0:T(1024)S(1)}, s32[4096]{0:T(1024)}, u32[]{:S(2)}) copy-start(s32[4096]{0:T(1024)} %param.9) | copy-start | bytes 49156
  7.6 5.7 %copy-start.2 = (s32[4096]{0:T(1024)S(1)}, s32[4096]{0:T(1024)}, u32[]{:S(2)}) copy-start(s32[4096]{0:T(1024)} %param.8) | copy-start | bytes 49156
  7.6 12.1 %collective-permute-start = (bf16[2,32,2048]{2,1,0:T(8,128)(2,1)S(1)}, bf16[2,32,2048]{2,1,0:T(8,128)(2,1)S(1)}, u32[]{:S(2)}, u32[]{:S(2)}) collective-permute-start(bf16[2,32,2048]{2,1,0:T(8,128)(2,1)S(1)} %get-tuple-element.25), channel_id=1, source_target_pairs={{0,1},{1,0},{2,3},{3,2},{4,5},{5,4},{6,7},{7,6},{8,9},{9,8},{10,11... | collective-permute-start | bytes 786440 | tf_op jit(solution)/shard_map/ppermute | solution.py:237
  13.2 24.2 %collective-permute-start.4 = (u16[128,2048]{1,0:T(8,128)(2,1)}, u16[128,2048]{1,0:T(8,128)(2,1)}, u32[]{:S(2)}, u32[]{:S(2)}) collective-permute-start(u16[128,2048]{1,0:T(8,128)(2,1)} %get-tuple-element.42), channel_id=1, source_target_pairs={{0,1},{1,0},{2,3},{3,2},{4,5},{5,4},{6,7},{7,6},{8,9},{9,8},{10,11... | collective-permute-start | bytes 1572872 | tf_op jit(solution)/shard_map/ppermute | solution.py:237
  20.5 54.8 %all-gather.7.cloned.1.call-start = ((), (), s32[]{:S(2)}) async-start(), calls=%async_computation.2 | async-start | bytes 1310720 | tf_op jit(solution)/shard_map/all_gather | solution.py:246
  22.7 18.3 %collective-permute-start.1 = (bf16[2,32,2048]{2,1,0:T(8,128)(2,1)}, bf16[2,32,2048]{2,1,0:T(8,128)(2,1)S(1)}, u32[]{:S(2)}, u32[]{:S(2)}) collective-permute-start(bf16[2,32,2048]{2,1,0:T(8,128)(2,1)} %get-tuple-element.53), channel_id=1, source_target_pairs={{0,1},{1,0},{2,3},{3,2},{4,5},{5,4},{6,7},{7,6},{8,9},{9,8},{10,11... | collective-permute-start | bytes 786440 | tf_op jit(solution)/shard_map/ppermute | solution.py:237
  24.7 16.4 %collective-permute-start.2 = (bf16[2,32,2048]{2,1,0:T(8,128)(2,1)}, bf16[2,32,2048]{2,1,0:T(8,128)(2,1)S(1)}, u32[]{:S(2)}, u32[]{:S(2)}) collective-permute-start(bf16[2,32,2048]{2,1,0:T(8,128)(2,1)} %get-tuple-element.52), channel_id=1, source_target_pairs={{0,2},{1,3},{2,0},{3,1},{4,6},{5,7},{6,4},{7,5},{8,10},{9,11},{10,... | collective-permute-start | bytes 786440 | tf_op jit(solution)/shard_map/ppermute | solution.py:237
  27.3 21.3 %collective-permute-start.3 = (bf16[2,32,2048]{2,1,0:T(8,128)(2,1)S(1)}, bf16[2,32,2048]{2,1,0:T(8,128)(2,1)S(1)}, u32[]{:S(2)}, u32[]{:S(2)}) collective-permute-start(bf16[2,32,2048]{2,1,0:T(8,128)(2,1)S(1)} %get-tuple-element.51), channel_id=1, source_target_pairs={{0,3},{1,2},{2,1},{3,0},{4,7},{5,6},{6,5},{7,4},{8,11},{9,10},{10,... | collective-permute-start | bytes 786440 | tf_op jit(solution)/shard_map/ppermute | solution.py:237
  29.1 65.1 %all-gather.9.cloned.1.call-start = ((), (), s32[]{:S(2)}) async-start(), calls=%async_computation.3 | async-start | bytes 1310720 | tf_op jit(solution)/shard_map/all_gather | solution.py:246
  37.4 29.9 %collective-permute-start.5 = (bf16[2,32,2048]{2,1,0:T(8,128)(2,1)S(1)}, bf16[2,32,2048]{2,1,0:T(8,128)(2,1)}, u32[]{:S(2)}, u32[]{:S(2)}) collective-permute-start(bf16[2,32,2048]{2,1,0:T(8,128)(2,1)S(1)} %get-tuple-element.37), channel_id=1, source_target_pairs={{0,1},{1,0},{2,3},{3,2},{4,5},{5,4},{6,7},{7,6},{8,9},{9,8},{10,11... | collective-permute-start | bytes 786440 | tf_op jit(solution)/shard_map/ppermute | solution.py:237
  39.5 9.0 %copy-start = (bf16[32,4096]{1,0:T(8,128)(2,1)S(1)}, bf16[32,4096]{1,0:T(8,128)(2,1)}, u32[]{:S(2)}) copy-start(bf16[32,4096]{1,0:T(8,128)(2,1)} %get-tuple-element.33.refs_10_) | copy-start | bytes 786436
  69.1 44.0 %all-gather.11.cloned.1.call-start = ((), (), s32[]{:S(2)}) async-start(), calls=%async_computation.4 | async-start | bytes 1310720 | tf_op jit(solution)/shard_map/all_gather | solution.py:246
  70.1 24.0 %collective-permute-start.6 = (bf16[2,32,2048]{2,1,0:T(8,128)(2,1)}, bf16[2,32,2048]{2,1,0:T(8,128)(2,1)S(1)}, u32[]{:S(2)}, u32[]{:S(2)}) collective-permute-start(bf16[2,32,2048]{2,1,0:T(8,128)(2,1)} %get-tuple-element.47), channel_id=1, source_target_pairs={{0,1},{1,0},{2,3},{3,2},{4,5},{5,4},{6,7},{7,6},{8,9},{9,8},{10,11... | collective-permute-start | bytes 786440 | tf_op jit(solution)/shard_map/ppermute | solution.py:237
  72.0 22.1 %collective-permute-start.7 = (bf16[2,32,2048]{2,1,0:T(8,128)(2,1)S(1)}, bf16[2,32,2048]{2,1,0:T(8,128)(2,1)S(1)}, u32[]{:S(2)}, u32[]{:S(2)}) collective-permute-start(bf16[2,32,2048]{2,1,0:T(8,128)(2,1)S(1)} %get-tuple-element.46), channel_id=1, source_target_pairs={{0,2},{1,3},{2,0},{3,1},{4,6},{5,7},{6,4},{7,5},{8,10},{9,11},{10,... | collective-permute-start | bytes 786440 | tf_op jit(solution)/shard_map/ppermute | solution.py:237
  73.0 21.1 %collective-permute-start.8 = (bf16[2,32,2048]{2,1,0:T(8,128)(2,1)S(1)}, bf16[2,32,2048]{2,1,0:T(8,128)(2,1)S(1)}, u32[]{:S(2)}, u32[]{:S(2)}) collective-permute-start(bf16[2,32,2048]{2,1,0:T(8,128)(2,1)S(1)} %get-tuple-element.45), channel_id=1, source_target_pairs={{0,3},{1,2},{2,1},{3,0},{4,7},{5,6},{6,5},{7,4},{8,11},{9,10},{10,... | collective-permute-start | bytes 786440 | tf_op jit(solution)/shard_map/ppermute | solution.py:237
Sparse Core Ops, SparseCore 0:
  20.6 18.3 all-gather.4
  40.6 16.7 all-gather.6
  69.2 17.2 all-gather.8
  87.9 16.7 all-gather.10
